TPU v7x, 32 devices: a whole 2x2x4 slice. The times are simulated.
32 devices in a mesh: samp: 8 (over z, y), var: 4 (over x, core).
Axes of the slice: x: 2, y: 2, z: 4, core: 2. Of those that a mesh axis runs over, the one named last changes fastest.
Arguments:
- genotypes: int32 [2048, 4096], P('samp', 'var'), may hold values from -1 to 2, as said below
- ancestry: float32 [16, 2048], P(None, 'samp'), may hold values from 0.05 to 4, as said below
- frequency: float32 [16, 4096], P(None, 'var'), may hold values from 0.05 to 0.95
Outputs:
- new_ancestry: float32 [16, 2048], P(None, 'samp')
- new_frequency: float32 [16, 4096], P(None, 'var')
Inputs may be any that keep to these rules, and one draw needn't show every extreme that they name: `genotypes`: A dosage of 0, 1 or 2 alternate alleles, or -1 for a missing genotype. `ancestry`: positive weights.
All inputs are finite; a program needn't handle non-finite values.
Results may differ from a plain program's by a relative error of at most 0.0003.
Values sent between devices are 32-bit elements; how exact they have to be, the bound alone decides.
A program may use at most 64 MiB of HBM per device.

v0:
```python
import jax
import jax.numpy as jnp
from jax import lax
from jax.sharding import PartitionSpec as P

ITERS = 4


HIGH = lax.Precision.HIGHEST


def contract(left, right, left_dim, right_dim):
    return lax.dot_general(
        left,
        right,
        (((left_dim,), (right_dim,)), ((), ())),
        precision=HIGH,
        preferred_element_type=jnp.float32,
    )


def shards(genotypes, ancestry, frequency):
    present = (genotypes >= 0).astype(jnp.float32)
    dosage = jnp.maximum(genotypes, 0).astype(jnp.float32)
    weight_ref = present * dosage
    weight_alt = present * (2.0 - dosage)
    fraction = ancestry / jnp.sum(ancestry, axis=0, keepdims=True)
    for sweep in range(ITERS):
        expected = contract(fraction, frequency, 0, 0)
        ratio_ref = weight_ref / expected
        ratio_alt = weight_alt / (1.0 - expected)
        partial_value = contract(frequency, ratio_ref, 1, 1) + contract(
            1.0 - frequency, ratio_alt, 1, 1
        )
        total = lax.psum(partial_value, "var")
        weighted = fraction * total
        fraction = weighted / jnp.sum(weighted, axis=0, keepdims=True)
        expected = contract(fraction, frequency, 0, 0)
        ratio_ref = weight_ref / expected
        ratio_alt = weight_alt / (1.0 - expected)
        term_ref = contract(fraction, ratio_ref, 1, 0)
        term_alt = contract(fraction, ratio_alt, 1, 0)
        sum_ref, sum_alt = lax.psum((term_ref, term_alt), "samp")
        upper = frequency * sum_ref
        lower = (1.0 - frequency) * sum_alt
        frequency = upper / (upper + lower)
    return (fraction, frequency)


def solution(mesh):
    return jax.shard_map(
        shards,
        mesh=mesh,
        in_specs=(P("samp", "var"), P(None, "samp"), P(None, "var")),
        out_specs=(P(None, "samp"), P(None, "var")),
        check_vma=False,
    )
```

profile of v0, /device:TPU:0, one launch (start us, length us, event | category | flops | bytes accessed | tf_op | source)
XLA Modules:
  0.0 370.3 jit_solution(9430064719370559565)
XLA Ops:
  7.2 0.0 copy-start.1
  7.2 0.0 copy-start.3
  7.2 0.0 all-reduce.15.cloned.1.call-start
  7.2 0.8 reduce_sum.45
  8.1 0.0 copy-start
  8.1 1.9 fusion.36
  10.0 1.1 convolution_bitcast_fusion
  11.1 1.1 convolution_add_fusion.3
  12.2 12.7 %psum.84 = f32[16,256]{1,0:T(8,128)S(1)} all-reduce(f32[16,256]{1,0:T(8,128)S(1)} %convolution_add_fusion.3), channel_id=1, replica_groups=mesh['samp'=8,'var'=4] {'var'}, use_global_device_ids=true, to_apply=%region_1.0 | all-reduce | flops 4096 | bytes 32768 | tf_op jit(solution)/shard_map/psum | solution.py:35
  24.9 1.0 fusion.52
  25.9 1.5 fusion.15
  27.5 1.5 fusion.12
  28.9 0.0 all-reduce.15.cloned.1.call-update
  29.0 0.0 all-reduce.13.cloned.1.call-start
  29.0 70.3 %all-reduce.15.cloned.1.call-done = (f32[16,1024]{1,0:T(8,128)}, f32[16,1024]{1,0:T(8,128)}) async-done(((f32[16,1024]{1,0:T(8,128)}, f32[16,1024]{1,0:T(8,128)}), (f32[16,1024]{1,0:T(8,128)}, f32[16,1024]{1,0:T(8,128)})) %all-reduce.15.cloned.1.call-update) | async-done | bytes 131088 | tf_op jit(solution)/shard_map/psum | solution.py:43
  99.3 0.9 add_divide_fusion.3
  100.2 1.0 fusion.53
  101.3 1.0 fusion.10
  102.3 1.1 convolution_add_fusion.2
  103.4 10.1 %psum.87 = f32[16,256]{1,0:T(8,128)S(1)} all-reduce(f32[16,256]{1,0:T(8,128)S(1)} %convolution_add_fusion.2), channel_id=1, replica_groups=mesh['samp'=8,'var'=4] {'var'}, use_global_device_ids=true, to_apply=%region_5.0 | all-reduce | flops 4096 | bytes 32768 | tf_op jit(solution)/shard_map/psum | solution.py:35
  113.5 1.0 fusion.48
  114.5 1.5 fusion.16
  116.1 1.5 fusion.8
  117.5 0.0 all-reduce.13.cloned.1.call-update
  117.6 0.2 all-reduce.11.cloned.1.call-start
  117.8 69.2 %all-reduce.13.cloned.1.call-done = (f32[16,1024]{1,0:T(8,128)}, f32[16,1024]{1,0:T(8,128)}) async-done(((f32[16,1024]{1,0:T(8,128)}, f32[16,1024]{1,0:T(8,128)}), (f32[16,1024]{1,0:T(8,128)}, f32[16,1024]{1,0:T(8,128)})) %all-reduce.13.cloned.1.call-update) | async-done | bytes 131088 | tf_op jit(solution)/shard_map/psum | solution.py:43
  187.0 0.9 add_divide_fusion.2
  187.8 1.0 fusion.47
  188.9 1.0 fusion.6
  189.9 1.1 convolution_add_fusion.1
  191.0 10.1 %psum.90 = f32[16,256]{1,0:T(8,128)S(1)} all-reduce(f32[16,256]{1,0:T(8,128)S(1)} %convolution_add_fusion.1), channel_id=1, replica_groups=mesh['samp'=8,'var'=4] {'var'}, use_global_device_ids=true, to_apply=%region_9.0 | all-reduce | flops 4096 | bytes 32768 | tf_op jit(solution)/shard_map/psum | solution.py:35
  201.1 1.0 fusion.54
  202.2 1.5 fusion.17
  203.7 1.5 fusion.4
  205.2 0.0 all-reduce.11.cloned.1.call-update
  205.2 0.0 all-reduce.9.cloned.1.call-start
  205.2 69.4 %all-reduce.11.cloned.1.call-done = (f32[16,1024]{1,0:T(8,128)}, f32[16,1024]{1,0:T(8,128)}) async-done(((f32[16,1024]{1,0:T(8,128)}, f32[16,1024]{1,0:T(8,128)}), (f32[16,1024]{1,0:T(8,128)}, f32[16,1024]{1,0:T(8,128)})) %all-reduce.11.cloned.1.call-update) | async-done | bytes 131088 | tf_op jit(solution)/shard_map/psum | solution.py:43
  274.6 0.9 add_divide_fusion.1
  275.5 1.0 fusion.55
  276.5 1.0 fusion.2
  277.6 1.1 convolution_add_fusion
  278.6 10.1 %psum.93 = f32[16,256]{1,0:T(8,128)S(1)} all-reduce(f32[16,256]{1,0:T(8,128)S(1)} %convolution_add_fusion), channel_id=1, replica_groups=mesh['samp'=8,'var'=4] {'var'}, use_global_device_ids=true, to_apply=%region_13.0 | all-reduce | flops 4096 | bytes 32768 | tf_op jit(solution)/shard_map/psum | solution.py:35
  288.8 1.0 fusion.56
  289.8 1.5 fusion.18
  291.4 1.5 fusion
  292.8 0.0 all-reduce.9.cloned.1.call-update
  292.9 69.4 %all-reduce.9.cloned.1.call-done = (f32[16,1024]{1,0:T(8,128)}, f32[16,1024]{1,0:T(8,128)}) async-done(((f32[16,1024]{1,0:T(8,128)}, f32[16,1024]{1,0:T(8,128)}), (f32[16,1024]{1,0:T(8,128)}, f32[16,1024]{1,0:T(8,128)})) %all-reduce.9.cloned.1.call-update) | async-done | bytes 131088 | tf_op jit(solution)/shard_map/psum | solution.py:43
  362.2 1.5 add_divide_fusion
  (12 shorter events, 0.1 us)
Async XLA Ops:
  7.2 0.9 copy-start.1
  7.2 2.8 copy-start.3
  7.2 92.1 %all-reduce.15.cloned.1.call-start = ((), (), s32[]{:S(2)}) async-start(), calls=%async_computation.3 | async-start | bytes 262144 | tf_op jit(solution)/shard_map/psum | solution.py:43
  8.1 2.0 copy-start
  29.0 158.0 %all-reduce.13.cloned.1.call-start = ((), (), s32[]{:S(2)}) async-start(), calls=%async_computation.2 | async-start | bytes 262144 | tf_op jit(solution)/shard_map/psum | solution.py:43
  117.6 157.1 %all-reduce.11.cloned.1.call-start = ((), (), s32[]{:S(2)}) async-start(), calls=%async_computation.1 | async-start | bytes 262144 | tf_op jit(solution)/shard_map/psum | solution.py:43
  205.2 157.1 %all-reduce.9.cloned.1.call-start = ((), (), s32[]{:S(2)}) async-start(), calls=%async_computation | async-start | bytes 262144 | tf_op jit(solution)/shard_map/psum | solution.py:43
  288.8 2.6 copy-start.2
Sparse Core Ops, SparseCore 0:
  29.1 70.2 all-reduce.14
  117.7 69.2 all-reduce.12
  205.3 69.2 all-reduce.10
  293.0 69.2 all-reduce.8
where the time goes:
time: 371 us; the launch traced here: 370 us
  waiting for transfers between devices  278 us (75%)
  blocking collectives  43 us (12%)
  matrix products  29.6 us (8%)
  between operations  13.9 us (4%)
  other arithmetic  5.13 us (1%)
    psum x4, waiting for transfers between devices, shards(): sum_ref, sum_alt = lax.psum((term_ref, term_alt), 'samp')  278 us
    psum x4, blocking collectives, shards(): total = lax.psum(partial_value, 'var')  43 us
    dot_general x24, matrix products, contract(): lax.dot_general(left, right, (((left_dim,), (right_dim,)), ((), ())), pre...  29.6 us
  transfers between devices with their start and end apart: 4, of which 4 were waited for; matrix products, arithmetic and copies ran while one was open for 0% of the time, Pallas kernels for 0%

commit v1 on v0

v1 whole, which is shorter than its diff:
```python
import functools

import jax
import jax.numpy as jnp
from jax import lax
from jax.experimental import pallas as pl
from jax.experimental.pallas import tpu as pltpu
from jax.sharding import PartitionSpec as P

ITERS = 4
MESH = pl.DeviceIdType.MESH
BF = jnp.bfloat16
F32 = jnp.float32


def rounded(x):
    return x.astype(BF).astype(F32)


def split3(x):
    x1 = rounded(x)
    rest = x - x1
    x2 = rounded(rest)
    x3 = rounded(rest - x2)
    return x1, x2, x3


def split2(x):
    hi = x.astype(BF)
    return hi, (x - hi.astype(F32)).astype(BF)


def dot(left, right, right_dim):
    return lax.dot_general(
        left, right, (((1,), (right_dim,)), ((), ())), preferred_element_type=F32
    )


def kernel(
    S, V, C, W, G,
    geno, anc, freq0, out_f, out_p,
    a_ref, b_ref, pcat, fbuf, qbuf, psrc, precv,
    q_send, q_recv, p_send, p_recv, g_send, g_recv,
):
    K, rows = anc.shape
    pairs = C // G
    width = W * G
    samp = lax.axis_index("samp")
    var = lax.axis_index("var")
    owner_only = S != C

    barrier = pltpu.get_barrier_semaphore()
    for d in range(1, S):
        pl.semaphore_signal(
            barrier, inc=1, device_id=(lax.rem(samp + d, S), var), device_id_type=MESH
        )
    for d in range(1, V):
        pl.semaphore_signal(
            barrier, inc=1, device_id=(samp, lax.rem(var + d, V)), device_id_type=MESH
        )

    def q_copy(s, slot, peer):
        return pltpu.make_async_remote_copy(
            src_ref=qbuf.at[s, slot], dst_ref=qbuf.at[s, slot],
            send_sem=q_send.at[s, peer], recv_sem=q_recv.at[s, slot],
            device_id=(samp, peer), device_id_type=MESH,
        )

    def p_copy(s, j, slot, peer):
        return pltpu.make_async_remote_copy(
            src_ref=psrc.at[s, j], dst_ref=precv.at[s, slot],
            send_sem=p_send.at[s, j], recv_sem=p_recv.at[s, slot],
            device_id=(peer, var), device_id_type=MESH,
        )

    def g_copy(s, slot, peer):
        return pltpu.make_async_remote_copy(
            src_ref=fbuf.at[s + 1, slot], dst_ref=fbuf.at[s + 1, slot],
            send_sem=g_send.at[s, peer], recv_sem=g_recv.at[s, slot],
            device_id=(peer, var), device_id_type=MESH,
        )

    def when_owner(f):
        if owner_only:
            pl.when(samp < C)(f)
        else:
            f()

    def columns(pair):
        return pl.ds(pl.multiple_of(pair * width, width), width)

    def prepare(pair):
        g = geno[:, columns(pair)]
        present = g >= 0
        a_ref[:, columns(pair)] = jnp.maximum(g, 0).astype(F32)
        b_ref[:, columns(pair)] = jnp.where(present, 2.0, 0.0)

    def fraction_rows(f):
        f1, f2, f3 = split3(f)
        stacked = jnp.concatenate([f1, f1, f2, f2, f1, f3, f2, f3], axis=0)
        return jnp.transpose(stacked).astype(BF)

    def frequency_of(s, pair):
        return jnp.concatenate([fbuf[s, pair * G + i] for i in range(G)], axis=1)

    own_pair = lax.rem(samp, C) // G

    for j in range(C):
        fbuf[0, j] = freq0[:, j * W:(j + 1) * W]
    f = anc[...]
    f = f / jnp.sum(f, axis=0, keepdims=True)
    count = None
    for s in range(ITERS):
        f_t = fraction_rows(f)
        total = jnp.zeros((2 * K, rows), F32)
        present_sum = jnp.zeros((8, rows), F32)
        for step in range(pairs):
            pair = lax.rem(own_pair + step, pairs)
            if s == 0:
                prepare(pair)
            else:
                for i in range(G):
                    j = pair * G + i

                    @pl.when(j != samp)
                    def _():
                        g_copy(s - 1, j, j).wait_recv()
            p1, p2, p3 = split3(frequency_of(s, pair))
            cat = jnp.concatenate([p1, p2, p1, p2, p3, p1, p3, p2], axis=0).astype(BF)
            pcat[pair] = cat
            e = dot(f_t, cat, 0)
            a = a_ref[:, columns(pair)]
            b = b_ref[:, columns(pair)]
            diff = (a - b * e) * pl.reciprocal(e * (1.0 - e))
            hi, lo = split2(diff)
            left = cat[: 2 * K]
            total = total + dot(left, hi, 1) + dot(left, lo, 1)
            if s == 0:
                present_sum = present_sum + dot(jnp.ones((8, width), BF), b.astype(BF), 1)
        mine = total[:K] + total[K:]
        qbuf[s, var, :K] = mine
        if s == 0:
            qbuf[s, var, K:] = present_sum
            pl.semaphore_wait(barrier, S - 1 + V - 1)
        for d in range(1, V):
            q_copy(s, var, lax.rem(var + d, V)).start()
        for d in range(1, V):
            peer = lax.rem(var + d, V)
            q_copy(s, peer, peer).wait_recv()
        big = qbuf[s, 0, :K]
        for v in range(1, V):
            big = big + qbuf[s, v, :K]
        if s == 0:
            count = qbuf[0, 0, K:K + 8]
            for v in range(1, V):
                count = count + qbuf[0, v, K:K + 8]
            count = 1.0 / count[:1]
        mean = jnp.sum(f * big, axis=0, keepdims=True)
        f = f + f * ((big - mean) * count)

        f_t = fraction_rows(f)
        f_hi, f_lo = split2(f)
        left = jnp.concatenate([f_hi, f_lo], axis=0)
        for step in range(pairs):
            pair = lax.rem(own_pair + 1 + step, pairs)
            e = dot(f_t, pcat[pair], 0)
            a = a_ref[:, columns(pair)]
            b = b_ref[:, columns(pair)]
            om = 1.0 - e
            inv = pl.reciprocal(e * om)
            ref_hi, ref_lo = split2(a * (om * inv))
            alt_hi, alt_lo = split2((b - a) * (e * inv))
            up = dot(left, ref_hi, 0) + dot(left, ref_lo, 0)
            low = dot(left, alt_hi, 0) + dot(left, alt_lo, 0)
            both = jnp.concatenate([up[:K] + up[K:], low[:K] + low[K:]], axis=0)
            for i in range(G):
                j = pair * G + i
                part = both[:, i * W:(i + 1) * W]
                psrc[s, j] = part

                @pl.when(j == samp)
                def _():
                    precv[s, samp] = part

                @pl.when(j != samp)
                def _():
                    p_copy(s, j, samp, j).start()

        @when_owner
        def _():
            for d in range(1, S):
                peer = lax.rem(samp + d, S)
                p_copy(s, 0, peer, peer).wait_recv()
            sums = precv[s, 0]
            for q in range(1, S):
                sums = sums + precv[s, q]
            old = fbuf[s, samp]
            upper = old * sums[:K]
            lower = (1.0 - old) * sums[K:]
            fbuf[s + 1, samp] = upper / (upper + lower)
            for d in range(1, S):
                g_copy(s, samp, lax.rem(samp + d, S)).start()

    out_f[...] = f
    for j in range(C):
        @pl.when(j != samp)
        def _():
            g_copy(ITERS - 1, j, j).wait_recv()
        out_p[:, j * W:(j + 1) * W] = fbuf[ITERS, j]

    for s in range(ITERS):
        for d in range(1, V):
            q_copy(s, var, lax.rem(var + d, V)).wait_send()
        for j in range(C):
            @pl.when(j != samp)
            def _():
                p_copy(s, j, samp, j).wait_send()

        @when_owner
        def _():
            for d in range(1, S):
                g_copy(s, samp, lax.rem(samp + d, S)).wait_send()


def shards(S, V, genotypes, ancestry, frequency):
    rows, cols = genotypes.shape
    K = ancestry.shape[0]
    W = max(128, cols // S)
    C = cols // W
    G = 2 if W == 128 and C % 2 == 0 else 1
    dma = pltpu.SemaphoreType.DMA
    vmem = pl.BlockSpec(memory_space=pltpu.VMEM)
    return pl.pallas_call(
        functools.partial(kernel, S, V, C, W, G),
        out_shape=(
            jax.ShapeDtypeStruct(ancestry.shape, F32),
            jax.ShapeDtypeStruct(frequency.shape, F32),
        ),
        in_specs=[vmem] * 3,
        out_specs=(vmem, vmem),
        scratch_shapes=[
            pltpu.VMEM((rows, cols), F32),
            pltpu.VMEM((rows, cols), F32),
            pltpu.VMEM((C // G, 8 * K, W * G), BF),
            pltpu.VMEM((ITERS + 1, C, K, W), F32),
            pltpu.VMEM((ITERS, V, K + 8, rows), F32),
            pltpu.VMEM((ITERS, C, 2 * K, W), F32),
            pltpu.VMEM((ITERS, S, 2 * K, W), F32),
            dma((ITERS, V)), dma((ITERS, V)),
            dma((ITERS, C)), dma((ITERS, S)),
            dma((ITERS, S)), dma((ITERS, C)),
        ],
        compiler_params=pltpu.CompilerParams(
            collective_id=0, has_side_effects=True, vmem_limit_bytes=40 * 2 ** 20
        ),
        cost_estimate=pl.CostEstimate(
            flops=2 * 4 * 8 * rows * cols * K,
            bytes_accessed=4 * rows * cols,
            transcendentals=8 * rows * cols,
        ),
        name="em_sweeps",
    )(genotypes, ancestry, frequency)


def solution(mesh):
    return jax.shard_map(
        functools.partial(shards, mesh.shape["samp"], mesh.shape["var"]),
        mesh=mesh,
        in_specs=(P("samp", "var"), P(None, "samp"), P(None, "var")),
        out_specs=(P(None, "samp"), P(None, "var")),
        check_vma=False,
    )
```

time: 371 us -> 66.2 us (0.18)
  waiting for transfers between devices: 278 us -> 0 us
  Pallas kernels: 0 us -> 61.3 us
  blocking collectives: 43 us -> 0 us
  matrix products: 29.6 us -> 0 us
  between operations: 13.9 us -> 0.65 us
  other arithmetic: 5.13 us -> 0 us
  local copies, waits for them, and re-layouts: 0.02 us -> 4.01 us
    psum x4 -> x0, waiting for transfers between devices: 278 us -> none  [shards(): sum_ref, sum_alt = lax.psum((term_ref, term_alt), 'samp')]
    pallas_call x0 -> x1, Pallas kernels: none -> 61.3 us  [shards(): pl.pallas_call(functools.partial(kernel, S, V, C, W, G), out_shape=(jax.S...]
    psum x4 -> x0, blocking collectives: 43 us -> none  [shards(): total = lax.psum(partial_value, 'var')]
    dot_general x24 -> x0, matrix products: 29.6 us -> none  [contract(): lax.dot_general(left, right, (((left_dim,), (right_dim,)), ((), ())), pre...]
    div x7 -> x0, other arithmetic: 4.23 us -> none  [the longest x4 4.19 us: shards(): frequency = upper / (upper + lower)]
    unnamed x8, local copies, waits for them, and re-layouts: 0.02 us -> 4.01 us
  transfers between devices with their start and end apart: 4 -> 0, of which waited for: 4 -> 0; matrix products, arithmetic and copies ran while one was open for 0% -> 0% of each run, Pallas kernels for 0% -> 0%
where the time goes in v1:
time: 66.2 us; the launch traced here: 65.9 us
  Pallas kernels  61.3 us (93%)
  local copies, waits for them, and re-layouts  4.01 us (6%)
    pallas_call x1, Pallas kernels, shards(): pl.pallas_call(functools.partial(kernel, S, V, C, W, G), out_shape=(jax.S...  61.3 us
    unnamed x8, local copies, waits for them, and re-layouts  4.01 us

profile of v1, /device:TPU:0, one launch (start us, length us, event | category | flops | bytes accessed | tf_op | source)
XLA Modules:
  0.0 65.9 jit_solution(9097179543144795673)
XLA Ops:
  0.6 0.0 copy-start
  0.6 1.2 %copy-done = s32[256,1024]{1,0:T(8,128)S(1)} copy-done((s32[256,1024]{1,0:T(8,128)S(1)}, s32[256,1024]{1,0:T(8,128)}, u32[]{:S(2)}) %copy-start) | copy-done | bytes 1048600
  1.9 0.0 copy-start.1
  1.9 0.8 %copy-done.1 = f32[16,1024]{1,0:T(8,128)S(1)} copy-done((f32[16,1024]{1,0:T(8,128)S(1)}, f32[16,1024]{1,0:T(8,128)}, u32[]{:S(2)}) %copy-start.1) | copy-done | bytes 65560
  2.7 0.0 copy-start.2
  2.7 0.7 %copy-done.2 = f32[16,256]{1,0:T(8,128)S(1)} copy-done((f32[16,256]{1,0:T(8,128)S(1)}, f32[16,256]{1,0:T(8,128)}, u32[]{:S(2)}) %copy-start.2) | copy-done | bytes 16408
  3.4 61.3 %em_sweeps.1 = (f32[16,256]{1,0:T(8,128)S(1)}, f32[16,1024]{1,0:T(8,128)S(1)}) custom-call(s32[256,1024]{1,0:T(8,128)S(1)} %copy-done, f32[16,256]{1,0:T(8,128)S(1)} %copy-done.2, f32[16,1024]{1,0:T(8,128)S(1)} %copy-done.1), custom_call_target="tpu_custom_call" | custom-call | flops 268435456 | bytes 1048576 | tf_op jit(solution)/shard_map/em_sweeps/pallas_call | solution.py:233
  64.7 0.6 copy.7
  65.3 0.6 copy.8
Async XLA Ops:
  0.6 1.2 %copy-start = (s32[256,1024]{1,0:T(8,128)S(1)}, s32[256,1024]{1,0:T(8,128)}, u32[]{:S(2)}) copy-start(s32[256,1024]{1,0:T(8,128)} %geno.1) | copy-start | bytes 3145732
  1.9 0.8 %copy-start.1 = (f32[16,1024]{1,0:T(8,128)S(1)}, f32[16,1024]{1,0:T(8,128)}, u32[]{:S(2)}) copy-start(f32[16,1024]{1,0:T(8,128)} %freq0.1) | copy-start | bytes 196612
  2.7 0.7 %copy-start.2 = (f32[16,256]{1,0:T(8,128)S(1)}, f32[16,256]{1,0:T(8,128)}, u32[]{:S(2)}) copy-start(f32[16,256]{1,0:T(8,128)} %anc.1) | copy-start | bytes 49156

commit v2 on v1

--- a/solution.py
+++ b/solution.py
@@ -37,17 +37,39 @@
 
 
 def kernel(
-    S, V, C, W, G,
-    geno, anc, freq0, out_f, out_p,
-    a_ref, b_ref, pcat, fbuf, qbuf, psrc, precv,
-    q_send, q_recv, p_send, p_recv, g_send, g_recv,
+    S, V, C, W,
+    geno_hbm, anc_hbm, freq_hbm, out_f, out_p,
+    geno, anc, a_ref, b_ref, pcat, fbuf, qbuf, psrc, precv,
+    in_sem, geno_sem, q_send, q_recv, p_send, p_recv, g_send, g_recv,
 ):
     K, rows = anc.shape
-    pairs = C // G
-    width = W * G
     samp = lax.axis_index("samp")
     var = lax.axis_index("var")
-    owner_only = S != C
+    first = (S - C) // 2
+    mine_id = samp - first
+    owner = jnp.logical_and(mine_id >= 0, mine_id < C)
+    half = C // 2
+    side, low_part = samp // (S // 2), lax.rem(samp, half)
+
+    def chunk(step):
+        return lax.rem(side + step // half, 2) * half + lax.rem(low_part + step % half, half)
+
+    loads = [pltpu.make_async_copy(anc_hbm, anc, in_sem.at[C])]
+    for j in range(C):
+        loads.append(
+            pltpu.make_async_copy(
+                freq_hbm.at[:, pl.ds(j * W, W)], fbuf.at[0, j], in_sem.at[j]
+            )
+        )
+    for load in loads:
+        load.start()
+
+    def geno_load(j):
+        at = pl.ds(pl.multiple_of(j * W, W), W)
+        return pltpu.make_async_copy(geno_hbm.at[:, at], geno.at[j], geno_sem.at[j])
+
+    for step in range(C):
+        geno_load(chunk(step)).start()
 
     barrier = pltpu.get_barrier_semaphore()
     for d in range(1, S):
@@ -80,33 +102,20 @@
             device_id=(peer, var), device_id_type=MESH,
         )
 
-    def when_owner(f):
-        if owner_only:
-            pl.when(samp < C)(f)
-        else:
-            f()
-
-    def columns(pair):
-        return pl.ds(pl.multiple_of(pair * width, width), width)
-
-    def prepare(pair):
-        g = geno[:, columns(pair)]
+    def prepare(j):
+        geno_load(j).wait()
+        g = geno[j]
         present = g >= 0
-        a_ref[:, columns(pair)] = jnp.maximum(g, 0).astype(F32)
-        b_ref[:, columns(pair)] = jnp.where(present, 2.0, 0.0)
+        a_ref[j] = jnp.maximum(g, 0).astype(F32)
+        b_ref[j] = jnp.where(present, 2.0, 0.0)
 
     def fraction_rows(f):
         f1, f2, f3 = split3(f)
         stacked = jnp.concatenate([f1, f1, f2, f2, f1, f3, f2, f3], axis=0)
         return jnp.transpose(stacked).astype(BF)
 
-    def frequency_of(s, pair):
-        return jnp.concatenate([fbuf[s, pair * G + i] for i in range(G)], axis=1)
-
-    own_pair = lax.rem(samp, C) // G
-
-    for j in range(C):
-        fbuf[0, j] = freq0[:, j * W:(j + 1) * W]
+    for load in loads:
+        load.wait()
     f = anc[...]
     f = f / jnp.sum(f, axis=0, keepdims=True)
     count = None
@@ -114,29 +123,27 @@
         f_t = fraction_rows(f)
         total = jnp.zeros((2 * K, rows), F32)
         present_sum = jnp.zeros((8, rows), F32)
-        for step in range(pairs):
-            pair = lax.rem(own_pair + step, pairs)
+        for step in range(C):
+            j = chunk(step)
             if s == 0:
-                prepare(pair)
+                prepare(j)
             else:
-                for i in range(G):
-                    j = pair * G + i
-
-                    @pl.when(j != samp)
-                    def _():
-                        g_copy(s - 1, j, j).wait_recv()
-            p1, p2, p3 = split3(frequency_of(s, pair))
+
+                @pl.when(j != mine_id)
+                def _():
+                    g_copy(s - 1, j, j).wait_recv()
+            p1, p2, p3 = split3(fbuf[s, j])
             cat = jnp.concatenate([p1, p2, p1, p2, p3, p1, p3, p2], axis=0).astype(BF)
-            pcat[pair] = cat
+            pcat[j] = cat
             e = dot(f_t, cat, 0)
-            a = a_ref[:, columns(pair)]
-            b = b_ref[:, columns(pair)]
+            a = a_ref[j]
+            b = b_ref[j]
             diff = (a - b * e) * pl.reciprocal(e * (1.0 - e))
             hi, lo = split2(diff)
             left = cat[: 2 * K]
             total = total + dot(left, hi, 1) + dot(left, lo, 1)
             if s == 0:
-                present_sum = present_sum + dot(jnp.ones((8, width), BF), b.astype(BF), 1)
+                present_sum = present_sum + dot(jnp.ones((8, W), BF), b.astype(BF), 1)
         mine = total[:K] + total[K:]
         qbuf[s, var, :K] = mine
         if s == 0:
@@ -161,11 +168,11 @@
         f_t = fraction_rows(f)
         f_hi, f_lo = split2(f)
         left = jnp.concatenate([f_hi, f_lo], axis=0)
-        for step in range(pairs):
-            pair = lax.rem(own_pair + 1 + step, pairs)
-            e = dot(f_t, pcat[pair], 0)
-            a = a_ref[:, columns(pair)]
-            b = b_ref[:, columns(pair)]
+        for step in range(C):
+            j = chunk(C - 1 - step)
+            e = dot(f_t, pcat[j], 0)
+            a = a_ref[j]
+            b = b_ref[j]
             om = 1.0 - e
             inv = pl.reciprocal(e * om)
             ref_hi, ref_lo = split2(a * (om * inv))
@@ -173,20 +180,17 @@
             up = dot(left, ref_hi, 0) + dot(left, ref_lo, 0)
             low = dot(left, alt_hi, 0) + dot(left, alt_lo, 0)
             both = jnp.concatenate([up[:K] + up[K:], low[:K] + low[K:]], axis=0)
-            for i in range(G):
-                j = pair * G + i
-                part = both[:, i * W:(i + 1) * W]
-                psrc[s, j] = part
-
-                @pl.when(j == samp)
-                def _():
-                    precv[s, samp] = part
-
-                @pl.when(j != samp)
-                def _():
-                    p_copy(s, j, samp, j).start()
-
-        @when_owner
+            psrc[s, j] = both
+
+            @pl.when(j == mine_id)
+            def _():
+                precv[s, samp] = both
+
+            @pl.when(j != mine_id)
+            def _():
+                p_copy(s, j, samp, first + j).start()
+
+        @pl.when(owner)
         def _():
             for d in range(1, S):
                 peer = lax.rem(samp + d, S)
@@ -194,16 +198,16 @@
             sums = precv[s, 0]
             for q in range(1, S):
                 sums = sums + precv[s, q]
-            old = fbuf[s, samp]
+            old = fbuf[s, mine_id]
             upper = old * sums[:K]
             lower = (1.0 - old) * sums[K:]
-            fbuf[s + 1, samp] = upper / (upper + lower)
+            fbuf[s + 1, mine_id] = upper / (upper + lower)
             for d in range(1, S):
-                g_copy(s, samp, lax.rem(samp + d, S)).start()
+                g_copy(s, mine_id, lax.rem(samp + d, S)).start()
 
     out_f[...] = f
     for j in range(C):
-        @pl.when(j != samp)
+        @pl.when(j != mine_id)
         def _():
             g_copy(ITERS - 1, j, j).wait_recv()
         out_p[:, j * W:(j + 1) * W] = fbuf[ITERS, j]
@@ -212,40 +216,42 @@
         for d in range(1, V):
             q_copy(s, var, lax.rem(var + d, V)).wait_send()
         for j in range(C):
-            @pl.when(j != samp)
+            @pl.when(j != mine_id)
             def _():
-                p_copy(s, j, samp, j).wait_send()
-
-        @when_owner
+                p_copy(s, j, samp, first + j).wait_send()
+
+        @pl.when(owner)
         def _():
             for d in range(1, S):
-                g_copy(s, samp, lax.rem(samp + d, S)).wait_send()
+                g_copy(s, mine_id, lax.rem(samp + d, S)).wait_send()
 
 
 def shards(S, V, genotypes, ancestry, frequency):
     rows, cols = genotypes.shape
     K = ancestry.shape[0]
-    W = max(128, cols // S)
-    C = cols // W
-    G = 2 if W == 128 and C % 2 == 0 else 1
+    C = 4
+    W = cols // C
     dma = pltpu.SemaphoreType.DMA
     vmem = pl.BlockSpec(memory_space=pltpu.VMEM)
     return pl.pallas_call(
-        functools.partial(kernel, S, V, C, W, G),
+        functools.partial(kernel, S, V, C, W),
         out_shape=(
             jax.ShapeDtypeStruct(ancestry.shape, F32),
             jax.ShapeDtypeStruct(frequency.shape, F32),
         ),
-        in_specs=[vmem] * 3,
+        in_specs=[pl.BlockSpec(memory_space=pltpu.HBM)] * 3,
         out_specs=(vmem, vmem),
         scratch_shapes=[
-            pltpu.VMEM((rows, cols), F32),
-            pltpu.VMEM((rows, cols), F32),
-            pltpu.VMEM((C // G, 8 * K, W * G), BF),
+            pltpu.VMEM((C, rows, W), jnp.int32),
+            pltpu.VMEM((K, rows), F32),
+            pltpu.VMEM((C, rows, W), F32),
+            pltpu.VMEM((C, rows, W), F32),
+            pltpu.VMEM((C, 8 * K, W), BF),
             pltpu.VMEM((ITERS + 1, C, K, W), F32),
             pltpu.VMEM((ITERS, V, K + 8, rows), F32),
             pltpu.VMEM((ITERS, C, 2 * K, W), F32),
             pltpu.VMEM((ITERS, S, 2 * K, W), F32),
+            dma((C + 1,)), dma((C,)),
             dma((ITERS, V)), dma((ITERS, V)),
             dma((ITERS, C)), dma((ITERS, S)),
             dma((ITERS, S)), dma((ITERS, C)),

time: 66.2 us -> 62.9 us (0.950)
  Pallas kernels: 61.3 us -> 58 us
    pallas_call x1, Pallas kernels: 61.3 us -> 58 us  [shards(): pl.pallas_call(functools.partial(kernel, S, V, C, W), out_shape=(jax.Shap...]
where the time goes in v2:
time: 62.9 us; the launch traced here: 62.6 us
  Pallas kernels  58 us (92%)
  local copies, waits for them, and re-layouts  4.01 us (6%)
  between operations  0.65 us (1%)
    pallas_call x1, Pallas kernels, shards(): pl.pallas_call(functools.partial(kernel, S, V, C, W), out_shape=(jax.Shap...  58 us
    unnamed x8, local copies, waits for them, and re-layouts  4.01 us

profile of v2, /device:TPU:0, one launch (start us, length us, event | category | flops | bytes accessed | tf_op | source)
XLA Modules:
  0.0 62.6 jit_solution(1722406944824998713)
XLA Ops:
  0.6 0.0 copy-start
  0.6 1.2 %copy-done = s32[256,1024]{1,0:T(8,128)S(1)} copy-done((s32[256,1024]{1,0:T(8,128)S(1)}, s32[256,1024]{1,0:T(8,128)}, u32[]{:S(2)}) %copy-start) | copy-done | bytes 1048600
  1.9 0.0 copy-start.1
  1.9 0.8 %copy-done.1 = f32[16,1024]{1,0:T(8,128)S(1)} copy-done((f32[16,1024]{1,0:T(8,128)S(1)}, f32[16,1024]{1,0:T(8,128)}, u32[]{:S(2)}) %copy-start.1) | copy-done | bytes 65560
  2.7 0.0 copy-start.2
  2.7 0.7 %copy-done.2 = f32[16,256]{1,0:T(8,128)S(1)} copy-done((f32[16,256]{1,0:T(8,128)S(1)}, f32[16,256]{1,0:T(8,128)}, u32[]{:S(2)}) %copy-start.2) | copy-done | bytes 16408
  3.4 58.0 %em_sweeps.1 = (f32[16,256]{1,0:T(8,128)S(1)}, f32[16,1024]{1,0:T(8,128)S(1)}) custom-call(s32[256,1024]{1,0:T(8,128)S(1)} %copy-done, f32[16,256]{1,0:T(8,128)S(1)} %copy-done.2, f32[16,1024]{1,0:T(8,128)S(1)} %copy-done.1), custom_call_target="tpu_custom_call" | custom-call | flops 268435456 | bytes 1048576 | tf_op jit(solution)/shard_map/em_sweeps/pallas_call | solution.py:236
  61.4 0.6 copy.7
  62.0 0.6 %copy.8 = f32[16,1024]{1,0:T(8,128)} copy(f32[16,1024]{1,0:T(8,128)S(1)} %get-tuple-element.5) | data formatting | bytes 131072
Async XLA Ops:
  0.6 1.2 %copy-start = (s32[256,1024]{1,0:T(8,128)S(1)}, s32[256,1024]{1,0:T(8,128)}, u32[]{:S(2)}) copy-start(s32[256,1024]{1,0:T(8,128)} %geno_hbm.1) | copy-start | bytes 3145732
  1.9 0.8 %copy-start.1 = (f32[16,1024]{1,0:T(8,128)S(1)}, f32[16,1024]{1,0:T(8,128)}, u32[]{:S(2)}) copy-start(f32[16,1024]{1,0:T(8,128)} %freq_hbm.1) | copy-start | bytes 196612
  2.7 0.7 %copy-start.2 = (f32[16,256]{1,0:T(8,128)S(1)}, f32[16,256]{1,0:T(8,128)}, u32[]{:S(2)}) copy-start(f32[16,256]{1,0:T(8,128)} %anc_hbm.1) | copy-start | bytes 49156

commit v3 on v2

--- a/solution.py
+++ b/solution.py
@@ -8,6 +8,8 @@
 from jax.sharding import PartitionSpec as P
 
 ITERS = 4
+Q_GROUPS = ((0,), (1,), (2,), (3,))
+P_GROUPS = ((3,), (2,), (1,), (0,))
 MESH = pl.DeviceIdType.MESH
 BF = jnp.bfloat16
 F32 = jnp.float32
@@ -65,11 +67,11 @@
         load.start()
 
     def geno_load(j):
-        at = pl.ds(pl.multiple_of(j * W, W), W)
-        return pltpu.make_async_copy(geno_hbm.at[:, at], geno.at[j], geno_sem.at[j])
+        at = pl.ds(j * (rows // C), rows // C)
+        return pltpu.make_async_copy(geno_hbm.at[at], geno.at[at], geno_sem.at[j])
 
     for step in range(C):
-        geno_load(chunk(step)).start()
+        geno_load(step).start()
 
     barrier = pltpu.get_barrier_semaphore()
     for d in range(1, S):
@@ -103,8 +105,7 @@
         )
 
     def prepare(j):
-        geno_load(j).wait()
-        g = geno[j]
+        g = geno[:, pl.ds(pl.multiple_of(j * W, W), W)]
         present = g >= 0
         a_ref[j] = jnp.maximum(g, 0).astype(F32)
         b_ref[j] = jnp.where(present, 2.0, 0.0)
@@ -116,34 +117,45 @@
 
     for load in loads:
         load.wait()
+    for step in range(C):
+        geno_load(step).wait()
     f = anc[...]
     f = f / jnp.sum(f, axis=0, keepdims=True)
     count = None
+    f_t = fraction_rows(f)
     for s in range(ITERS):
-        f_t = fraction_rows(f)
         total = jnp.zeros((2 * K, rows), F32)
         present_sum = jnp.zeros((8, rows), F32)
-        for step in range(C):
-            j = chunk(step)
-            if s == 0:
-                prepare(j)
-            else:
-
-                @pl.when(j != mine_id)
-                def _():
-                    g_copy(s - 1, j, j).wait_recv()
-            p1, p2, p3 = split3(fbuf[s, j])
-            cat = jnp.concatenate([p1, p2, p1, p2, p3, p1, p3, p2], axis=0).astype(BF)
-            pcat[j] = cat
-            e = dot(f_t, cat, 0)
-            a = a_ref[j]
-            b = b_ref[j]
-            diff = (a - b * e) * pl.reciprocal(e * (1.0 - e))
-            hi, lo = split2(diff)
-            left = cat[: 2 * K]
-            total = total + dot(left, hi, 1) + dot(left, lo, 1)
-            if s == 0:
-                present_sum = present_sum + dot(jnp.ones((8, W), BF), b.astype(BF), 1)
+        for group in Q_GROUPS:
+            chunks = [chunk(step) for step in group]
+            for j in chunks:
+                if s == 0:
+                    prepare(j)
+                else:
+
+                    @pl.when(j != mine_id)
+                    def _():
+                        g_copy(s - 1, j, j).wait_recv()
+            cats, diffs = [], []
+            for j in chunks:
+                p1, p2, p3 = split3(fbuf[s, j])
+                cats.append(
+                    jnp.concatenate([p1, p2, p1, p2, p3, p1, p3, p2], axis=0).astype(BF)
+                )
+            for j, cat in zip(chunks, cats):
+                e = dot(f_t, cat, 0)
+                diffs.append(
+                    ((a_ref[j] - b_ref[j] * e) * pl.reciprocal(e * (1.0 - e))).astype(BF)
+                )
+            for j, cat, diff in zip(chunks, cats, diffs):
+                left = cat[: 2 * K]
+                total = total + dot(left, diff, 1)
+                if s == 0:
+                    present_sum = present_sum + dot(
+                        jnp.ones((8, W), BF), b_ref[j].astype(BF), 1
+                    )
+            for j, cat in zip(chunks, cats):
+                pcat[j] = cat
         mine = total[:K] + total[K:]
         qbuf[s, var, :K] = mine
         if s == 0:
@@ -168,27 +180,34 @@
         f_t = fraction_rows(f)
         f_hi, f_lo = split2(f)
         left = jnp.concatenate([f_hi, f_lo], axis=0)
-        for step in range(C):
-            j = chunk(C - 1 - step)
-            e = dot(f_t, pcat[j], 0)
-            a = a_ref[j]
-            b = b_ref[j]
-            om = 1.0 - e
-            inv = pl.reciprocal(e * om)
-            ref_hi, ref_lo = split2(a * (om * inv))
-            alt_hi, alt_lo = split2((b - a) * (e * inv))
-            up = dot(left, ref_hi, 0) + dot(left, ref_lo, 0)
-            low = dot(left, alt_hi, 0) + dot(left, alt_lo, 0)
-            both = jnp.concatenate([up[:K] + up[K:], low[:K] + low[K:]], axis=0)
-            psrc[s, j] = both
-
-            @pl.when(j == mine_id)
-            def _():
-                precv[s, samp] = both
-
-            @pl.when(j != mine_id)
-            def _():
-                p_copy(s, j, samp, first + j).start()
+        for group in P_GROUPS:
+            chunks = [chunk(step) for step in group]
+            ratios = []
+            for j in chunks:
+                e = dot(f_t, pcat[j], 0)
+                a = a_ref[j]
+                om = 1.0 - e
+                inv = pl.reciprocal(e * om)
+                ratios.append(
+                    (split2(a * (om * inv)), split2((b_ref[j] - a) * (e * inv)))
+                )
+            sums = []
+            for (ref_hi, ref_lo), (alt_hi, alt_lo) in ratios:
+                up = dot(left, ref_hi, 0) + dot(left, ref_lo, 0)
+                low = dot(left, alt_hi, 0) + dot(left, alt_lo, 0)
+                sums.append(
+                    jnp.concatenate([up[:K] + up[K:], low[:K] + low[K:]], axis=0)
+                )
+            for j, both in zip(chunks, sums):
+                psrc[s, j] = both
+
+                @pl.when(j == mine_id)
+                def _():
+                    precv[s, samp] = both
+
+                @pl.when(j != mine_id)
+                def _():
+                    p_copy(s, j, samp, first + j).start()
 
         @pl.when(owner)
         def _():
@@ -202,7 +221,7 @@
             upper = old * sums[:K]
             lower = (1.0 - old) * sums[K:]
             fbuf[s + 1, mine_id] = upper / (upper + lower)
-            for d in range(1, S):
+            for d in range(S - 1, 0, -1):
                 g_copy(s, mine_id, lax.rem(samp + d, S)).start()
 
     out_f[...] = f
@@ -242,7 +261,7 @@
         in_specs=[pl.BlockSpec(memory_space=pltpu.HBM)] * 3,
         out_specs=(vmem, vmem),
         scratch_shapes=[
-            pltpu.VMEM((C, rows, W), jnp.int32),
+            pltpu.VMEM((rows, cols), jnp.int32),
             pltpu.VMEM((K, rows), F32),
             pltpu.VMEM((C, rows, W), F32),
             pltpu.VMEM((C, rows, W), F32),

time: 62.9 us -> 62.6 us (level)
  no operation moved by 1% of the time
where the time goes in v3:
time: 62.6 us; the launch traced here: 62.4 us
  Pallas kernels  57.7 us (92%)
  local copies, waits for them, and re-layouts  4.01 us (6%)
  between operations  0.65 us (1%)
    pallas_call x1, Pallas kernels, shards(): pl.pallas_call(functools.partial(kernel, S, V, C, W), out_shape=(jax.Shap...  57.7 us
    unnamed x8, local copies, waits for them, and re-layouts  4.01 us

profile of v3, /device:TPU:0, one launch (start us, length us, event | category | flops | bytes accessed | tf_op | source)
XLA Modules:
  0.0 62.4 jit_solution(18429405575000759823)
XLA Ops:
  0.6 0.0 copy-start
  0.6 1.2 %copy-done = s32[256,1024]{1,0:T(8,128)S(1)} copy-done((s32[256,1024]{1,0:T(8,128)S(1)}, s32[256,1024]{1,0:T(8,128)}, u32[]{:S(2)}) %copy-start) | copy-done | bytes 1048600
  1.9 0.0 copy-start.1
  1.9 0.8 %copy-done.1 = f32[16,1024]{1,0:T(8,128)S(1)} copy-done((f32[16,1024]{1,0:T(8,128)S(1)}, f32[16,1024]{1,0:T(8,128)}, u32[]{:S(2)}) %copy-start.1) | copy-done | bytes 65560
  2.7 0.0 copy-start.2
  2.7 0.7 %copy-done.2 = f32[16,256]{1,0:T(8,128)S(1)} copy-done((f32[16,256]{1,0:T(8,128)S(1)}, f32[16,256]{1,0:T(8,128)}, u32[]{:S(2)}) %copy-start.2) | copy-done | bytes 16408
  3.4 57.7 %em_sweeps.1 = (f32[16,256]{1,0:T(8,128)S(1)}, f32[16,1024]{1,0:T(8,128)S(1)}) custom-call(s32[256,1024]{1,0:T(8,128)S(1)} %copy-done, f32[16,256]{1,0:T(8,128)S(1)} %copy-done.2, f32[16,1024]{1,0:T(8,128)S(1)} %copy-done.1), custom_call_target="tpu_custom_call" | custom-call | flops 268435456 | bytes 1048576 | tf_op jit(solution)/shard_map/em_sweeps/pallas_call | solution.py:255
  61.1 0.6 copy.7
  61.8 0.6 %copy.8 = f32[16,1024]{1,0:T(8,128)} copy(f32[16,1024]{1,0:T(8,128)S(1)} %get-tuple-element.5) | data formatting | bytes 131072
Async XLA Ops:
  0.6 1.2 %copy-start = (s32[256,1024]{1,0:T(8,128)S(1)}, s32[256,1024]{1,0:T(8,128)}, u32[]{:S(2)}) copy-start(s32[256,1024]{1,0:T(8,128)} %geno_hbm.1) | copy-start | bytes 3145732
  1.9 0.8 %copy-start.1 = (f32[16,1024]{1,0:T(8,128)S(1)}, f32[16,1024]{1,0:T(8,128)}, u32[]{:S(2)}) copy-start(f32[16,1024]{1,0:T(8,128)} %freq_hbm.1) | copy-start | bytes 196612
  2.7 0.7 %copy-start.2 = (f32[16,256]{1,0:T(8,128)S(1)}, f32[16,256]{1,0:T(8,128)}, u32[]{:S(2)}) copy-start(f32[16,256]{1,0:T(8,128)} %anc_hbm.1) | copy-start | bytes 49156
